TPU v7x, 32 devices: a whole 2x2x4 slice. The times are simulated.
32 devices in a mesh: groups: 2 (over x), expert: 16 (over z, y, core).
Axes of the slice: x: 2, y: 2, z: 4, core: 2. Of those that a mesh axis runs over, the one named last changes fastest.
Arguments:
- acts: bfloat16 [4096, 2048], P(('groups', 'expert')), parts along dimension 0, may hold values from -6 to 6
- out_grad: bfloat16 [4096, 2048], P(('groups', 'expert')), parts along dimension 0, may hold values from -6 to 6
- routes: int32 [4096, 8], P(('groups', 'expert')), parts along dimension 0, may hold values from 0 to 15, all different within a row; in each aligned block of 128 rows (0 to 127, 128 to 255, ...) at most 128 rows name the same one
- route_weight: float32 [4096, 8], P(('groups', 'expert')), parts along dimension 0, may hold values from 0.05 to 1
- w_gate: bfloat16 [16, 2048, 768], P('expert'), may hold values from -0.125 to 0.125
- w_up: bfloat16 [16, 2048, 768], P('expert'), may hold values from -0.125 to 0.125
- proj_in: bfloat16 [16, 768, 32], P('expert'), may hold values from -4 to 4
- proj_out: bfloat16 [2048, 32], replicated, may hold values from -0.125 to 0.125
Outputs:
- sketches: float32 [16, 4, 1024], P('expert', 'groups'), parts along dimension 1
There are 2 independent parts, one for each index of `groups`. A program takes and returns all parts, laid end to end along the dimension named above; an argument that names none is the same for every part. Nothing has to cross between parts.
Inputs may be any that keep to these rules, and one draw needn't show every extreme that they name: `routes`: in the 128 tokens of one device (an aligned block) no expert is named by more than 128 tokens, a bound that some block reaches; a token names 8 different experts.
All inputs are finite; a program needn't handle non-finite values.
Results may differ from a plain program's by a relative error of at most 0.005.
Values may be sent and summed in bfloat16 or wider, within the bound.
A program may use at most 128 MiB of HBM per device.

v0:
```python
import jax
import jax.numpy as jnp
from jax import lax
from jax.sharding import PartitionSpec as P

EXAMPLES = 2


def on_device(acts, out_grad, routes, route_weight, w_gate, w_up, proj_in, proj_out):
    sources = lax.axis_size("expert")
    tok_count = acts.shape[0]
    top_count = routes.shape[1]
    model_width = acts.shape[1]
    side = proj_out.shape[1]
    capacity = max(2, 2 * tok_count * top_count // sources)
    flat_dest = routes.reshape(-1)
    onehot = (flat_dest[:, None] == jnp.arange(sources, dtype=jnp.int32)[None, :]).astype(jnp.int32)
    earlier = jnp.cumsum(onehot, axis=0) - onehot
    slot_index = jnp.sum(earlier * onehot, axis=1)
    target = flat_dest * capacity + slot_index
    token_of = jnp.arange(tok_count * top_count, dtype=jnp.int32) // top_count
    send_rows = (
        jnp.zeros((sources * capacity, model_width), jnp.bfloat16).at[target].set(acts[token_of])
    )
    send_rows = send_rows.reshape(sources, capacity, model_width)
    scaled = (route_weight.reshape(-1)[:, None] * out_grad[token_of].astype(jnp.float32)).astype(
        jnp.bfloat16
    )
    projected = jnp.dot(scaled, proj_out, preferred_element_type=jnp.float32).astype(jnp.bfloat16)
    grad_rows = jnp.zeros((sources * capacity, side), jnp.bfloat16).at[target].set(projected)
    grad_rows = grad_rows.reshape(sources, capacity, side)
    rows = lax.all_to_all(send_rows, "expert", split_axis=0, concat_axis=0, tiled=True)
    grads = lax.all_to_all(grad_rows, "expert", split_axis=0, concat_axis=0, tiled=True)
    gate = jnp.einsum("scd,df->scf", rows, w_gate[0], preferred_element_type=jnp.float32)
    upper = jnp.einsum("scd,df->scf", rows, w_up[0], preferred_element_type=jnp.float32)
    hidden = (jax.nn.silu(gate) * upper).astype(jnp.bfloat16)
    reduced = jnp.einsum("scf,fr->scr", hidden, proj_in[0], preferred_element_type=jnp.float32)
    grad_side = grads
    reduced, grad_side = (reduced, grad_side)
    per_source = jnp.einsum(
        "sci,scj->sij", reduced, grad_side.astype(jnp.float32), precision=lax.Precision.HIGHEST
    )
    span = sources // EXAMPLES
    raw = per_source.reshape(EXAMPLES, span, side * side).sum(axis=1)
    power = lax.psum(jnp.sum(raw * raw, axis=1), "expert")
    factor = lax.rsqrt(power / (sources * side * side) + 1e-06)
    return (raw * factor[:, None])[None]


def solution(mesh):
    return jax.shard_map(
        on_device,
        mesh=mesh,
        in_specs=(
            P(("groups", "expert"), None),
            P(("groups", "expert"), None),
            P(("groups", "expert"), None),
            P(("groups", "expert"), None),
            P("expert", None, None),
            P("expert", None, None),
            P("expert", None, None),
            P(),
        ),
        out_specs=P("expert", "groups", None),
        check_vma=False,
    )
```

profile of v0, /device:TPU:0, one launch (start us, length us, event | category | flops | bytes accessed | tf_op | source)
XLA Modules:
  0.0 287.5 jit_solution(10173910662498937413)
XLA Ops:
  0.0 0.0 copy-start
  0.0 0.9 copy.12
  0.9 0.1 eq.29
  1.0 0.1 eq.25
  1.1 0.7 broadcast_multiply_fusion
  1.8 4.5 %reduce-window.6 = s32[16,8,128]{2,1,0:T(8,128)S(1)} reduce-window(s32[16,8,128]{2,1,0:T(8,128)S(1)} %fusion.17, s32[]{:T(128)} %constant.31.clone.1), window={size=1x1x128 pad=0_0x0_0x127_0}, to_apply=%region_0.0 | reduce-window | flops 2080768 | bytes 131076 | tf_op jit(solution)/shard_map/reduce-window
  6.4 0.1 slice.12
  6.4 0.1 copy.14
  6.6 0.1 copy.15
  6.7 0.1 broadcast_add_fusion
  6.8 0.1 copy.11
  6.9 0.1 mul.52
  7.0 25.5 %scatter_custom_fusion = bf16[2048,2048]{1,0:T(8,128)(2,1)} fusion(s32[1024]{0:T(1024)S(1)} %bitcast.50, bf16[128,2048]{1,0:T(8,128)(2,1)} %param.8, s32[1024]{0:T(1024)S(1)} %broadcast_clamp_fusion, bf16[]{:T(256)} %constant.29.clone.1), kind=kCustom, calls=%fused_computation.7 | custom fusion | bytes 8389120 | tf_op jit(solution)/shard_map/scatter | solution.py:23
  32.5 7.4 %all-to-all-start = ((bf16[16,128,2048]{2,1,0:T(8,128)(2,1)}), bf16[16,128,2048]{2,1,0:T(8,128)(2,1)}, u32[]{:S(2)}, u32[]{:S(2)}) async-start(bf16[16,128,2048]{2,1,0:T(8,128)(2,1)} %bitcast.44), calls=%async_computation | async-start | bytes 16777216 | tf_op jit(solution)/shard_map/all_to_all | solution.py:32
  40.0 0.0 copy-start.1
  40.0 0.0 copy-start.2
  40.0 10.0 %gather_fusion = bf16[1024,2048]{1,0:T(8,128)(2,1)} fusion(bf16[128,2048]{1,0:T(8,128)(2,1)} %param.9, s32[1024]{0:T(1024)S(1)} %broadcast_clamp_fusion), kind=kCustom, calls=%fused_computation.1 | custom fusion | bytes 8392704 | tf_op jit(solution)/shard_map/gather | solution.py:26
  50.0 0.0 copy-done.1
  50.0 0.1 copy.16
  50.1 0.1 mul.56
  50.2 0.0 copy-done.2
  50.2 3.6 %fusion.11 = bf16[1024,32]{0,1:T(8,128)(2,1)S(1)} fusion(bf16[2048,32]{0,1:T(8,128)(2,1)S(1)} %copy-done.2, bf16[1024,2048]{1,0:T(8,128)(2,1)} %gather_fusion, f32[1024]{0:T(1024)S(1)} %mul.56), kind=kOutput, calls=%fused_computation.15 | convolution fusion | flops 140541952 | bytes 4395008 | tf_op jit(solution)/shard_map/dot_general | solution.py:29
  53.8 0.2 copy.17
  54.0 4.0 %scatter_custom_fusion.1 = bf16[2048,32]{1,0:T(8,128)(2,1)} fusion(s32[1024]{0:T(1024)S(1)} %bitcast.51, bf16[1024,32]{1,0:T(8,128)(2,1)S(1)} %copy.17, bf16[]{:T(256)} %constant.29.clone.1), kind=kCustom, calls=%fused_computation.16 | custom fusion | bytes 131074 | tf_op jit(solution)/shard_map/scatter | solution.py:30
  58.0 1.9 copy.19
  59.9 130.8 %all-to-all-done = bf16[16,128,2048]{2,1,0:T(8,128)(2,1)} async-done(((bf16[16,128,2048]{2,1,0:T(8,128)(2,1)}), bf16[16,128,2048]{2,1,0:T(8,128)(2,1)}, u32[]{:S(2)}, u32[]{:S(2)}) %all-to-all-start) | async-done | bytes 8388640 | tf_op jit(solution)/shard_map/all_to_all | solution.py:32
  190.7 36.5 %all-to-all-start.1 = ((bf16[16,128,32]{1,2,0:T(8,128)(2,1)}), bf16[16,128,32]{1,2,0:T(8,128)(2,1)S(1)}, u32[]{:S(2)}, u32[]{:S(2)}) async-start(bf16[16,128,32]{1,2,0:T(8,128)(2,1)} %copy.19), calls=%async_computation.1 | async-start | bytes 262144 | tf_op jit(solution)/shard_map/all_to_all | solution.py:33
  227.2 0.0 copy-done
  227.2 0.0 copy-start.3
  227.2 10.7 %fusion.5 = f32[16,128,768]{2,1,0:T(8,128)} fusion(bf16[16,128,2048]{2,1,0:T(8,128)(2,1)} %all-to-all-done, bf16[1,2048,768]{2,1,0:T(8,128)(2,1)S(1)} %copy-done), kind=kOutput, calls=%fused_computation.11 | convolution fusion | flops 6442450944 | bytes 17825792 | tf_op jit(solution)/shard_map/scd,df->scf/dot_general | solution.py:35
  237.9 0.0 copy-done.3
  238.0 13.4 %fusion.9 = f32[16,128,32]{1,2,0:T(8,128)} fusion(f32[16,128,768]{2,1,0:T(8,128)} %fusion.5, bf16[16,128,2048]{2,1,0:T(8,128)(2,1)} %all-to-all-done, bf16[1,2048,768]{2,1,0:T(8,128)(2,1)} %param.12, bf16[1,768,32]{1,2,0:T(8,128)(2,1)S(1)} %copy-done.3), kind=kOutput, calls=%fused_computation.14 | convolution fusion | flops 6552551424 | bytes 18137088 | tf_op jit(solution)/shard_map/scf,fr->scr/dot_general | solution.py:37
  251.4 0.0 all-to-all-done.1
  251.4 1.3 fusion.20
  252.6 0.1 reshape.127
  252.8 0.1 multiply_reduce_fusion
  252.9 33.8 %psum.7 = f32[2]{0:T(128)S(1)} all-reduce(f32[2]{0:T(128)S(1)} %multiply_reduce_fusion), channel_id=1, replica_groups=mesh['groups'=2,'expert'=16] {'expert'}, use_global_device_ids=true, to_apply=%region_7.8 | all-reduce | flops 2 | bytes 16 | tf_op jit(solution)/shard_map/psum | solution.py:45
  286.8 0.7 bitcast_multiply_fusion
  (9 shorter events, 0.1 us)
Async XLA Ops:
  0.0 227.2 %copy-start = (bf16[1,2048,768]{2,1,0:T(8,128)(2,1)S(1)}, bf16[1,2048,768]{2,1,0:T(8,128)(2,1)}, u32[]{:S(2)}) copy-start(bf16[1,2048,768]{2,1,0:T(8,128)(2,1)} %param.13) | copy-start | bytes 9437188
  32.5 158.2 %all-to-all-start = ((bf16[16,128,2048]{2,1,0:T(8,128)(2,1)}), bf16[16,128,2048]{2,1,0:T(8,128)(2,1)}, u32[]{:S(2)}, u32[]{:S(2)}) async-start(bf16[16,128,2048]{2,1,0:T(8,128)(2,1)} %bitcast.44), calls=%async_computation | async-start | bytes 16777216 | tf_op jit(solution)/shard_map/all_to_all | solution.py:32
  40.0 10.0 %copy-start.1 = (f32[128,8]{0,1:T(8,128)S(1)}, f32[128,8]{0,1:T(8,128)}, u32[]{:S(2)}) copy-start(f32[128,8]{0,1:T(8,128)} %param.11) | copy-start | bytes 12292
  40.0 10.2 %copy-start.2 = (bf16[2048,32]{0,1:T(8,128)(2,1)S(1)}, bf16[2048,32]{0,1:T(8,128)(2,1)}, u32[]{:S(2)}) copy-start(bf16[2048,32]{0,1:T(8,128)(2,1)} %param.15) | copy-start | bytes 393220
  190.7 60.7 %all-to-all-start.1 = ((bf16[16,128,32]{1,2,0:T(8,128)(2,1)}), bf16[16,128,32]{1,2,0:T(8,128)(2,1)S(1)}, u32[]{:S(2)}, u32[]{:S(2)}) async-start(bf16[16,128,32]{1,2,0:T(8,128)(2,1)} %copy.19), calls=%async_computation.1 | async-start | bytes 262144 | tf_op jit(solution)/shard_map/all_to_all | solution.py:33
  227.2 10.7 %copy-start.3 = (bf16[1,768,32]{1,2,0:T(8,128)(2,1)S(1)}, bf16[1,768,32]{1,2,0:T(8,128)(2,1)}, u32[]{:S(2)}) copy-start(bf16[1,768,32]{1,2,0:T(8,128)(2,1)} %param.14) | copy-start | bytes 147460
where the time goes:
time: 288 us; the launch traced here: 287 us
  waiting for transfers between devices  131 us (45%)
  starting transfers between devices  43.9 us (15%)
  local copies, waits for them, and re-layouts  43.5 us (15%)
  blocking collectives  33.8 us (12%)
  matrix products  29 us (10%)
  other arithmetic  6.22 us (2%)
    all_to_all x1, waiting for transfers between devices, on_device(): lax.all_to_all(send_rows, 'expert', split_axis=0, concat_axis=0, tiled=True)  131 us
    all_to_all x1, starting transfers between devices, on_device(): lax.all_to_all(grad_rows, 'expert', split_axis=0, concat_axis=0, tiled=True)  36.5 us
    psum x1, blocking collectives, on_device(): power = lax.psum(jnp.sum(raw * raw, axis=1), 'expert')  33.8 us
    scatter x1, local copies, waits for them, and re-layouts, on_device(): jnp.zeros((sources * capacity, model_width), jnp.bfloat16).at[target]  25.5 us
    dot_general x1, matrix products, on_device(): jnp.einsum('scf,fr->scr', hidden, proj_in[0], preferred_element_type=jnp....  13.4 us
    dot_general x1, matrix products, on_device(): jnp.einsum('scd,df->scf', rows, w_up[0], preferred_element_type=jnp.float32)  10.7 us
    gather x1, local copies, waits for them, and re-layouts, on_device(): out_grad[token_of].astype(jnp.float32)  9.98 us
    all_to_all x1, starting transfers between devices, on_device(): lax.all_to_all(send_rows, 'expert', split_axis=0, concat_axis=0, tiled=True)  7.44 us
  transfers between devices with their start and end apart: 2, of which 1 were waited for; matrix products, arithmetic and copies ran while one was open for 15% of the time, Pallas kernels for 0%

commit v1 on v0

v1 whole, which is shorter than its diff:
```python
import functools

import jax
import jax.numpy as jnp
from jax import lax
from jax.experimental import pallas as pl
from jax.experimental.pallas import tpu as pltpu
from jax.sharding import PartitionSpec as P

EXAMPLES = 2
MESH = pl.DeviceIdType.MESH
RIGHT, LEFT, ACROSS, SIBLING = 0, 1, 2, 3


def row_chunks(rows, lines):
    half = rows // 2
    if lines == 1:
        return ((0, half), (half, rows - half)), 2
    late = rows // 8
    return ((0, half), (half, rows - half - late), (rows - late, late)), 2


def kernel(
    devices, lines, acts_ref, grad_ref, routes_ref, weight_ref, gate_ref, up_ref, in_ref, out_ref,
    result_ref,
    acts, grad, routes, weight, gate, up, proj_in, proj_out,
    sides_out, sides, total, powers,
    local_sem, arrive_sem, send_sem, side_arrive, side_send, power_arrive, power_send,
):
    length = devices // 2 // lines
    chips = devices // 2
    rows = acts.shape[1]
    side = sides.shape[1]
    width = gate.shape[1]
    top = routes.shape[1]
    chunks, first_count = row_chunks(rows, lines)
    me = lax.axis_index("expert")
    core = lax.rem(me, 2)
    chip = me // 2
    line = lax.rem(chip, lines)
    place = chip // lines

    def block(at_place, at_line, at_core):
        return (jnp.clip(at_place, 0, length - 1) * lines + at_line) * 2 + at_core

    def sibling_of(index):
        return index + 1 - 2 * lax.rem(index, 2)

    loads = [
        pltpu.make_async_copy(grad_ref, grad, local_sem.at[0]),
        pltpu.make_async_copy(out_ref, proj_out, local_sem.at[1]),
        pltpu.make_async_copy(routes_ref, routes, local_sem.at[2]),
        pltpu.make_async_copy(weight_ref, weight, local_sem.at[3]),
        pltpu.make_async_copy(acts_ref, acts.at[me], local_sem.at[4]),
        pltpu.make_async_copy(gate_ref.at[0], gate, local_sem.at[5]),
        pltpu.make_async_copy(up_ref.at[0], up, local_sem.at[6]),
        pltpu.make_async_copy(in_ref.at[0], proj_in, local_sem.at[7]),
    ]
    for load in loads:
        load.start()

    barrier = pltpu.get_barrier_semaphore()

    @pl.loop(1, devices)
    def _(i):
        other = lax.rem(me + i, devices)
        pl.semaphore_signal(barrier, inc=1, device_id={"expert": other}, device_id_type=MESH)

    pl.semaphore_wait(barrier, devices - 1)

    targets = (
        block(place + 1, line, core),
        block(place - 1, line, core),
        block(place, lines - 1 - line, core),
        sibling_of(me),
    )
    has_right = place < length - 1
    has_left = place > 0
    other_line = lines - 1 - line

    def transfer(index, chunk, way, own=False):
        start, count = chunks[chunk]
        rows_of = pl.ds(start, count)
        source = acts_ref.at[rows_of] if own else acts.at[index, rows_of]
        return pltpu.make_async_remote_copy(
            src_ref=source,
            dst_ref=acts.at[index, rows_of],
            send_sem=send_sem.at[way, index, chunk],
            recv_sem=arrive_sem.at[index, chunk],
            device_id={"expert": targets[way]},
            device_id_type=MESH,
        )

    def own_moves():
        moves = []
        for chunk in range(first_count, len(chunks)):
            moves.append((True, me, chunk, ACROSS))
        for chunk in range(len(chunks)):
            moves.append((has_right, me, chunk, RIGHT))
            moves.append((has_left, me, chunk, LEFT))
            if chunk < first_count and lines > 1:
                moves.append((True, me, chunk, ACROSS))
            moves.append((True, me, chunk, SIBLING))
        return moves

    def arrivals(distance):
        listed = []
        for chunk in range(first_count, len(chunks)):
            present = distance == 1
            index = block(place, other_line, core)
            moves = [
                (present & has_right, index, chunk, RIGHT),
                (present & has_left, index, chunk, LEFT),
                (present, index, chunk, SIBLING),
            ]
            listed.append((present, index, chunk, moves))
        for chunk in range(len(chunks)):
            late = chunk >= first_count
            for way in (RIGHT, LEFT):
                at = place - distance if way == RIGHT else place + distance
                inside = (at >= 0) if way == RIGHT else (at < length)
                onward = has_right if way == RIGHT else has_left
                present = (distance >= 1) & inside & (distance < length)
                index = block(at, line, core)
                moves = [(present & onward, index, chunk, way)]
                if lines > 1 and not late:
                    moves.append((present, index, chunk, ACROSS))
                moves.append((present, index, chunk, SIBLING))
                listed.append((present, index, chunk, moves))
                if lines == 1:
                    continue
                if late:
                    index = block(at, other_line, core)
                    moves = [(present & onward, index, chunk, way), (present, index, chunk, SIBLING)]
                    listed.append((present, index, chunk, moves))
                back = distance - 1
                at = place - back if way == RIGHT else place + back
                inside = (at >= 0) if way == RIGHT else (at < length)
                index = block(at, other_line, core)
                if not late:
                    present = (distance >= 1) & inside
                    if way == LEFT:
                        present = present & (back >= 1)
                    listed.append((present, index, chunk, [(present, index, chunk, SIBLING)]))
        return listed

    for present, index, chunk, way in own_moves():
        @pl.when(present)
        def _(index=index, chunk=chunk, way=way):
            transfer(index, chunk, way, own=True).start()

    for load in loads[:4]:
        load.wait()
    projected = jnp.dot(grad[...], proj_out[...], preferred_element_type=jnp.float32).T
    names = routes[...].astype(jnp.float32).T
    scales = weight[...].T

    @pl.loop(0, devices)
    def _(expert):
        hit = names == lax.convert_element_type(expert, jnp.float32)
        scale = jnp.sum(jnp.where(hit, scales, 0.0), axis=0, keepdims=True)
        sides_out[expert] = (projected * scale).astype(jnp.bfloat16)

    def side_move(other):
        return pltpu.make_async_remote_copy(
            src_ref=sides_out.at[other],
            dst_ref=sides.at[me],
            send_sem=side_send.at[other],
            recv_sem=side_arrive.at[me],
            device_id={"expert": other},
            device_id_type=MESH,
        )

    @pl.loop(1, devices)
    def _(i):
        side_move(lax.rem(me + i, devices)).start()

    sides[me] = sides_out[me]
    total[...] = jnp.zeros_like(total)
    for load in loads[4:]:
        load.wait()

    def compute(chip_index):
        x = acts[pl.ds(2 * chip_index, 2)].reshape(2 * rows, acts.shape[2])
        pair = sides[pl.ds(2 * chip_index, 2)]
        pair = jnp.concatenate([pair[0], pair[1]], axis=1)
        example = chip_index // (chips // EXAMPLES)
        step = 256
        for start in range(0, width, step):
            gated = jnp.dot(x, gate[:, start : start + step], preferred_element_type=jnp.float32)
            upper = jnp.dot(x, up[:, start : start + step], preferred_element_type=jnp.float32)
            hidden = (gated / (1.0 + jnp.exp(-gated)) * upper).astype(jnp.bfloat16)
            total[example, :, start : start + step] += jnp.dot(
                pair, hidden, preferred_element_type=jnp.float32
            )

    @pl.loop(0, length + (1 if lines > 1 else 0))
    def _(distance):
        for present, index, chunk, moves in arrivals(distance):
            @pl.when(present)
            def _(index=index, chunk=chunk):
                transfer(index, chunk, SIBLING).wait_recv()

            for wanted, index, chunk, way in moves:
                @pl.when(wanted)
                def _(index=index, chunk=chunk, way=way):
                    transfer(index, chunk, way).start()

        @pl.loop(0, 4 if lines > 1 else 2)
        def _(unit):
            partner = unit // 2
            leftward = lax.rem(unit, 2)
            far = distance - partner
            at = place - far + 2 * far * leftward
            present = (far >= leftward) & (at >= 0) & (at < length)
            index = block(at, line + partner * (other_line - line), core)

            @pl.when(present)
            def _():
                for chunk in range(len(chunks)):
                    transfer(sibling_of(index), chunk, SIBLING).wait_recv()

                pltpu.make_async_copy(
                    sides.at[sibling_of(index)],
                    sides.at[sibling_of(index)],
                    side_arrive.at[sibling_of(index)],
                ).wait()

                @pl.when(index != me)
                def _():
                    pltpu.make_async_copy(
                        sides.at[index], sides.at[index], side_arrive.at[index]
                    ).wait()

                compute(index // 2)

    raw = []
    matrix = proj_in[...].astype(jnp.float32)
    for example in range(EXAMPLES):
        turned = jnp.dot(
            total[example],
            matrix,
            preferred_element_type=jnp.float32,
            precision=lax.Precision.HIGHEST,
        )
        raw.append(turned.T)
    own_power = [jnp.sum(one * one, keepdims=True) for one in raw]
    row_of = lax.broadcasted_iota(jnp.int32, (8, 128), 0)
    tile = jnp.zeros((8, 128), jnp.float32)
    for example in range(EXAMPLES):
        tile = jnp.where(row_of == example, own_power[example], tile)
    powers[me] = tile

    def power_move(other):
        return pltpu.make_async_remote_copy(
            src_ref=powers.at[me],
            dst_ref=powers.at[me],
            send_sem=power_send.at[other],
            recv_sem=power_arrive.at[me],
            device_id={"expert": other},
            device_id_type=MESH,
        )

    @pl.loop(1, devices)
    def _(i):
        power_move(lax.rem(me + i, devices)).start()

    for present, index, chunk, way in own_moves():
        @pl.when(present)
        def _(index=index, chunk=chunk, way=way):
            transfer(index, chunk, way, own=True).wait_send()

    @pl.loop(0, length + (1 if lines > 1 else 0))
    def _(distance):
        for _, _, _, moves in arrivals(distance):
            for wanted, index, chunk, way in moves:
                @pl.when(wanted)
                def _(index=index, chunk=chunk, way=way):
                    transfer(index, chunk, way).wait_send()

    @pl.loop(1, devices)
    def _(i):
        other = lax.rem(me + i, devices)
        side_move(other).wait_send()
        power_move(other).wait_send()
        pltpu.make_async_copy(powers.at[other], powers.at[other], power_arrive.at[other]).wait()

    power = jnp.sum(powers[...], axis=0)
    factor = lax.rsqrt(power / (devices * side * side) + 1e-06)
    for example in range(EXAMPLES):
        result_ref[example] = raw[example] * factor[example : example + 1, :1]


def on_device(devices, lines, acts, out_grad, routes, route_weight, w_gate, w_up, proj_in, proj_out):
    rows, depth = acts.shape
    top = routes.shape[1]
    width = w_gate.shape[2]
    side = proj_out.shape[1]
    pieces = len(row_chunks(rows, lines)[0])
    dma = pltpu.SemaphoreType.DMA
    scaled = pl.pallas_call(
        functools.partial(kernel, devices, lines),
        out_shape=jax.ShapeDtypeStruct((EXAMPLES, side, side), jnp.float32),
        in_specs=[pl.BlockSpec(memory_space=pl.ANY)] * 8,
        out_specs=pl.BlockSpec(memory_space=pltpu.VMEM),
        scratch_shapes=[
            pltpu.VMEM((devices, rows, depth), jnp.bfloat16),
            pltpu.VMEM((rows, depth), jnp.bfloat16),
            pltpu.VMEM((rows, top), jnp.int32),
            pltpu.VMEM((rows, top), jnp.float32),
            pltpu.VMEM((depth, width), jnp.bfloat16),
            pltpu.VMEM((depth, width), jnp.bfloat16),
            pltpu.VMEM((width, side), jnp.bfloat16),
            pltpu.VMEM((depth, side), jnp.bfloat16),
            pltpu.VMEM((devices, side, rows), jnp.bfloat16),
            pltpu.VMEM((devices, side, rows), jnp.bfloat16),
            pltpu.VMEM((EXAMPLES, side, width), jnp.float32),
            pltpu.VMEM((devices, 8, 128), jnp.float32),
            dma((8,)),
            dma((devices, pieces)),
            dma((4, devices, pieces)),
            dma((devices,)),
            dma((devices,)),
            dma((devices,)),
            dma((devices,)),
        ],
        compiler_params=pltpu.CompilerParams(
            collective_id=0, has_side_effects=True, vmem_limit_bytes=60 * 1024 * 1024
        ),
        cost_estimate=pl.CostEstimate(
            flops=2 * devices * rows * depth * 2 * width,
            bytes_accessed=2 * depth * width * 2,
            transcendentals=devices * rows * width,
        ),
    )(acts, out_grad, routes, route_weight, w_gate, w_up, proj_in, proj_out)
    return scaled.reshape(1, EXAMPLES, side * side)


def solution(mesh):
    devices = mesh.shape["expert"]
    lines = 2 if devices == 16 else 1
    return jax.shard_map(
        functools.partial(on_device, devices, lines),
        mesh=mesh,
        in_specs=(
            P(("groups", "expert"), None),
            P(("groups", "expert"), None),
            P(("groups", "expert"), None),
            P(("groups", "expert"), None),
            P("expert", None, None),
            P("expert", None, None),
            P("expert", None, None),
            P(),
        ),
        out_specs=P("expert", "groups", None),
        check_vma=False,
    )
```

time: 288 us -> 71.5 us (0.25)
  waiting for transfers between devices: 131 us -> 0 us
  Pallas kernels: 0 us -> 63.4 us
  starting transfers between devices: 43.9 us -> 0 us
  local copies, waits for them, and re-layouts: 43.5 us -> 7.75 us
  blocking collectives: 33.8 us -> 0 us
  matrix products: 29 us -> 0 us
  other arithmetic: 6.22 us -> 0 us
    all_to_all x2 -> x0, waiting for transfers between devices: 131 us -> none  [the longest x1 131 us: on_device(): lax.all_to_all(send_rows, 'expert', split_axis=0, concat_axis=0, tiled=True)]
    pallas_call x0 -> x1, Pallas kernels: none -> 63.4 us  [on_device(): pl.pallas_call(functools.partial(kernel, devices, lines), out_shape=jax.S...]
    all_to_all x2 -> x0, starting transfers between devices: 43.9 us -> none  [the longest x1 36.5 us: on_device(): lax.all_to_all(grad_rows, 'expert', split_axis=0, concat_axis=0, tiled=True)]
    psum x1 -> x0, blocking collectives: 33.8 us -> none  [on_device(): power = lax.psum(jnp.sum(raw * raw, axis=1), 'expert')]
    scatter x2 -> x0, local copies, waits for them, and re-layouts: 29.5 us -> none  [the longest x1 25.5 us: on_device(): jnp.zeros((sources * capacity, model_width), jnp.bfloat16).at[target]]
    dot_general x4 -> x0, matrix products: 29 us -> none  [the longest x1 13.4 us: on_device(): jnp.einsum('scf,fr->scr', hidden, proj_in[0], preferred_element_type=jnp....]
    gather x1 -> x0, local copies, waits for them, and re-layouts: 9.98 us -> none  [on_device(): out_grad[token_of].astype(jnp.float32)]
    unnamed x10 -> x4, local copies, waits for them, and re-layouts: 1.06 us -> 6.31 us
  transfers between devices with their start and end apart: 2 -> 0, of which waited for: 1 -> 0; matrix products, arithmetic and copies ran while one was open for 15% -> 0% of each run, Pallas kernels for 0% -> 0%
where the time goes in v1:
time: 71.5 us; the launch traced here: 71.2 us
  Pallas kernels  63.4 us (89%)
  local copies, waits for them, and re-layouts  7.75 us (11%)
    pallas_call x1, Pallas kernels, on_device(): pl.pallas_call(functools.partial(kernel, devices, lines), out_shape=jax.S...  63.4 us
    unnamed x4, local copies, waits for them, and re-layouts  6.31 us
    reshape x1, local copies, waits for them, and re-layouts, on_device(): return scaled.reshape(1, EXAMPLES, side * side)  1.44 us

profile of v1, /device:TPU:0, one launch (start us, length us, event | category | flops | bytes accessed | tf_op | source)
XLA Modules:
  0.0 71.2 jit_solution(15416976493702596072)
XLA Ops:
  0.0 1.4 %copy.9.routes_ref = s32[128,8]{1,0:T(8,128)} copy(s32[128,8]{0,1:T(8,128)} %param.10) | data formatting | bytes 8192 | tf_op args[2]
  1.4 1.4 %copy.10.weight_ref = f32[128,8]{1,0:T(8,128)} copy(f32[128,8]{0,1:T(8,128)} %param.11) | data formatting | bytes 8192 | tf_op args[3]
  2.8 1.6 %copy.11.in_ref = bf16[1,768,32]{2,1,0:T(8,128)(2,1)} copy(bf16[1,768,32]{1,2,0:T(8,128)(2,1)} %param.14) | data formatting | bytes 98304 | tf_op args[6]
  4.4 1.9 %copy.12.out_ref = bf16[2048,32]{1,0:T(8,128)(2,1)} copy(bf16[2048,32]{0,1:T(8,128)(2,1)} %param.15) | data formatting | bytes 262144 | tf_op args[7]
  6.3 63.4 %shard_map.82 = f32[2,32,32]{2,1,0:T(8,128)} custom-call(bf16[128,2048]{1,0:T(8,128)(2,1)} %acts_ref.1, bf16[128,2048]{1,0:T(8,128)(2,1)} %grad_ref.1, s32[128,8]{1,0:T(8,128)} %copy.9.routes_ref, f32[128,8]{1,0:T(8,128)} %copy.10.weight_ref, bf16[1,2048,768]{2,1,0:T(8,128)(2,1)} %gate_ref.1, bf16[1,2048,768]{2,1,0:T(8,128)(2,1)} %up_ref.1, ...), custom_call_target="tpu_custom_call" | custom-call | flops 12884901888 | bytes 6291456 | tf_op jit(solution)/shard_map/pallas_call | solution.py:301
  69.8 1.4 %reshape.3 = f32[1,2,1024]{2,1,0:T(2,128)} reshape(f32[2,32,32]{2,1,0:T(8,128)} %shard_map.82) | data formatting | bytes 16384 | tf_op jit(solution)/shard_map/reshape | solution.py:336

commit v2 on v1

v2 whole, which is shorter than its diff:
```python
import functools

import jax
import jax.numpy as jnp
from jax import lax
from jax.experimental import pallas as pl
from jax.experimental.pallas import tpu as pltpu
from jax.sharding import PartitionSpec as P

EXAMPLES = 2
MESH = pl.DeviceIdType.MESH
RIGHT, LEFT, ACROSS, SIBLING = 0, 1, 2, 3


def row_chunks(rows, lines):
    part = rows // 4
    if lines == 1:
        return tuple((part * i, part) for i in range(4)), 4
    late = rows // 8
    first = rows - late - 2 * part
    return ((0, first), (first, part), (first + part, part), (rows - late, late)), 3


def kernel(
    devices, lines, acts_ref, grad_ref, routes_ref, weight_ref, gate_ref, up_ref, in_ref, out_ref,
    result_ref,
    acts, grad, routes, weight, gate, up, proj_in, proj_out,
    notes, total, powers,
    local_sem, arrive_sem, send_sem, power_arrive, power_send,
):
    length = devices // 2 // lines
    chips = devices // 2
    rows = acts.shape[1]
    side = proj_out.shape[0]
    width = gate.shape[1]
    chunks, first_count = row_chunks(rows, lines)
    me = lax.axis_index("expert")
    core = lax.rem(me, 2)
    chip = me // 2
    line = lax.rem(chip, lines)
    place = chip // lines

    def block(at_place, at_line, at_core):
        return (jnp.clip(at_place, 0, length - 1) * lines + at_line) * 2 + at_core

    def sibling_of(index):
        return index + 1 - 2 * lax.rem(index, 2)

    loads = [
        pltpu.make_async_copy(acts_ref, acts.at[me], local_sem.at[4]),
        pltpu.make_async_copy(grad_ref, grad, local_sem.at[0]),
        pltpu.make_async_copy(out_ref, proj_out, local_sem.at[1]),
        pltpu.make_async_copy(routes_ref, routes, local_sem.at[2]),
        pltpu.make_async_copy(weight_ref, weight, local_sem.at[3]),
        pltpu.make_async_copy(gate_ref.at[0], gate, local_sem.at[5]),
        pltpu.make_async_copy(up_ref.at[0], up, local_sem.at[6]),
        pltpu.make_async_copy(in_ref.at[0], proj_in, local_sem.at[7]),
    ]
    for load in loads:
        load.start()

    targets = (
        block(place + 1, line, core),
        block(place - 1, line, core),
        block(place, lines - 1 - line, core),
        sibling_of(me),
    )
    has_right = place < length - 1
    has_left = place > 0
    other_line = lines - 1 - line

    neighbours = [(has_right, RIGHT), (has_left, LEFT), (True, SIBLING)]
    if lines > 1:
        neighbours.append((True, ACROSS))
    barrier = pltpu.get_barrier_semaphore()
    for present, way in neighbours:
        @pl.when(present)
        def _(way=way):
            pl.semaphore_signal(
                barrier, inc=1, device_id={"expert": targets[way]}, device_id_type=MESH
            )

    loads[0].wait()
    others = 1 + (lines - 1) + has_right.astype(jnp.int32) + has_left.astype(jnp.int32)
    pl.semaphore_wait(barrier, others)

    notes_chunk = len(chunks)

    def transfer(index, chunk, way):
        if chunk == notes_chunk:
            moved = notes.at[index]
        else:
            start, count = chunks[chunk]
            moved = acts.at[index, pl.ds(start, count)]
        return pltpu.make_async_remote_copy(
            src_ref=moved,
            dst_ref=moved,
            send_sem=send_sem.at[way, index, chunk],
            recv_sem=arrive_sem.at[index, chunk],
            device_id={"expert": targets[way]},
            device_id_type=MESH,
        )

    def arrivals(distance, step):
        listed = []
        own = distance == 0
        for chunk in (step,) if step < notes_chunk - 1 else (step, notes_chunk):
            late = first_count <= chunk < notes_chunk
            if chunk == 0:
                for after in range(first_count, len(chunks)):
                    listed.append((False, me, after, [(own, me, after, ACROSS)]))
            for way in (RIGHT, LEFT):
                at = place - distance if way == RIGHT else place + distance
                onward = has_right if way == RIGHT else has_left
                inside = (distance >= 0) & ((at >= 0) if way == RIGHT else (at < length))
                inside = inside & (distance < length)
                once = inside if way == RIGHT else inside & (distance >= 1)
                index = block(at, line, core)
                moves = [(inside & onward, index, chunk, way)]
                if lines > 1 and not late:
                    moves.append((once, index, chunk, ACROSS))
                moves.append((once, index, chunk, SIBLING))
                listed.append((inside & (distance >= 1), index, chunk, moves))
            if lines == 1:
                continue
            for way in (RIGHT, LEFT):
                onward = has_right if way == RIGHT else has_left
                if late:
                    at = place - distance if way == RIGHT else place + distance
                    inside = (distance >= 0) & ((at >= 0) if way == RIGHT else (at < length))
                    inside = inside & (distance < length)
                    once = inside if way == RIGHT else inside & (distance >= 1)
                    index = block(at, other_line, core)
                    moves = [(inside & onward, index, chunk, way), (once, index, chunk, SIBLING)]
                    listed.append((once, index, chunk, moves))
                else:
                    back = distance - 1
                    at = place - back if way == RIGHT else place + back
                    inside = (at >= 0) if way == RIGHT else (at < length)
                    inside = inside & (back >= (0 if way == RIGHT else 1)) & (back < length)
                    index = block(at, other_line, core)
                    listed.append((inside, index, chunk, [(inside, index, chunk, SIBLING)]))
        return listed

    def project():
        for load in loads[1:5]:
            load.wait()
        projected = lax.dot_general(
            proj_out[...], grad[...], (((1,), (1,)), ((), ())), preferred_element_type=jnp.float32
        )
        names = routes[...]
        scales = weight[...]
        notes[me, :side] = projected
        for expert in range(devices):
            hit = names == expert
            notes[me, side + expert : side + expert + 1] = jnp.sum(
                jnp.where(hit, scales, 0.0), axis=0, keepdims=True
            )
        total[...] = jnp.zeros_like(total)
        for load in loads[5:]:
            load.wait()

    def compute(chip_index):
        x = acts[pl.ds(2 * chip_index, 2)].reshape(2 * rows, acts.shape[2])
        pair = [
            notes[2 * chip_index + part, :side] * notes[2 * chip_index + part, pl.ds(side + me, 1)]
            for part in range(2)
        ]
        pair = jnp.concatenate(pair, axis=1).astype(jnp.bfloat16)
        example = chip_index // (chips // EXAMPLES)
        step = 256
        for start in range(0, width, step):
            gated = jnp.dot(x, gate[:, start : start + step], preferred_element_type=jnp.float32)
            upper = jnp.dot(x, up[:, start : start + step], preferred_element_type=jnp.float32)
            hidden = (gated / (1.0 + jnp.exp(-gated)) * upper).astype(jnp.bfloat16)
            total[example, :, start : start + step] += jnp.dot(
                pair, hidden, preferred_element_type=jnp.float32
            )

    def wait_sent(distance, step, ways):
        for _, _, _, moves in arrivals(distance, step):
            for wanted, index, chunk, way in moves:
                if way in ways:
                    @pl.when(wanted)
                    def _(index=index, chunk=chunk, way=way):
                        transfer(index, chunk, way).wait_send()

    steps = len(chunks)
    last = length + (1 if lines > 1 else 0)

    @pl.loop(0, last + 1)
    def _(distance):
        for step in range(steps):
            if step == 2:
                pl.when(distance == 0)(project)
            before = distance if step >= 2 else distance - 1
            wait_sent(before, (step - 2) % steps, (RIGHT, LEFT, ACROSS))
            for present, index, chunk, moves in arrivals(distance, step):
                if present is not False:
                    @pl.when(present)
                    def _(index=index, chunk=chunk):
                        transfer(index, chunk, SIBLING).wait_recv()

                for wanted, index, chunk, way in moves:
                    @pl.when(wanted)
                    def _(index=index, chunk=chunk, way=way):
                        transfer(index, chunk, way).start()

            if step >= (4 if lines > 1 else 2):
                continue
            partner = step // 2
            far = distance - 1 - partner
            at = place + far if step % 2 else place - far
            present = (far >= step % 2) & (at >= 0) & (at < length)
            index = block(at, other_line if partner else line, core)

            @pl.when(present)
            def _(index=index):
                for chunk in range(len(chunks) + 1):
                    transfer(sibling_of(index), chunk, SIBLING).wait_recv()

                compute(index // 2)

    raw = []
    matrix = proj_in[...].astype(jnp.float32)
    for example in range(EXAMPLES):
        raw.append(
            lax.dot_general(
                matrix,
                total[example],
                (((1,), (1,)), ((), ())),
                preferred_element_type=jnp.float32,
                precision=lax.Precision.HIGHEST,
            )
        )
    own_power = [jnp.sum(one * one, keepdims=True) for one in raw]
    row_of = lax.broadcasted_iota(jnp.int32, (8, 128), 0)
    tile = jnp.zeros((8, 128), jnp.float32)
    for example in range(EXAMPLES):
        tile = jnp.where(row_of == example, own_power[example], tile)
    powers[me] = tile

    def power_move(other):
        return pltpu.make_async_remote_copy(
            src_ref=powers.at[me],
            dst_ref=powers.at[me],
            send_sem=power_send.at[other],
            recv_sem=power_arrive.at[me],
            device_id={"expert": other},
            device_id_type=MESH,
        )

    for i in range(1, devices):
        power_move(lax.rem(me + i, devices)).start()

    @pl.loop(0, last)
    def _(distance):
        for step in range(steps):
            wait_sent(distance, step, (SIBLING,))

    for i in range(1, devices):
        other = lax.rem(me + i, devices)
        power_move(other).wait_send()
        pltpu.make_async_copy(powers.at[other], powers.at[other], power_arrive.at[other]).wait()

    power = jnp.sum(powers[...], axis=0)
    factor = lax.rsqrt(power / (devices * side * side) + 1e-06)
    for example in range(EXAMPLES):
        result_ref[example] = raw[example] * factor[example : example + 1, :1]


def on_device(devices, lines, acts, out_grad, routes, route_weight, w_gate, w_up, proj_in, proj_out):
    rows, depth = acts.shape
    top = routes.shape[1]
    width = w_gate.shape[2]
    side = proj_out.shape[1]
    pieces = len(row_chunks(rows, lines)[0]) + 1
    dma = pltpu.SemaphoreType.DMA
    scaled = pl.pallas_call(
        functools.partial(kernel, devices, lines),
        out_shape=jax.ShapeDtypeStruct((EXAMPLES, side, side), jnp.float32),
        in_specs=[pl.BlockSpec(memory_space=pl.ANY)] * 8,
        out_specs=pl.BlockSpec(memory_space=pltpu.VMEM),
        scratch_shapes=[
            pltpu.VMEM((devices, rows, depth), jnp.bfloat16),
            pltpu.VMEM((rows, depth), jnp.bfloat16),
            pltpu.VMEM((top, rows), jnp.int32),
            pltpu.VMEM((top, rows), jnp.float32),
            pltpu.VMEM((depth, width), jnp.bfloat16),
            pltpu.VMEM((depth, width), jnp.bfloat16),
            pltpu.VMEM((side, width), jnp.bfloat16),
            pltpu.VMEM((side, depth), jnp.bfloat16),
            pltpu.VMEM((devices, side + devices, rows), jnp.float32),
            pltpu.VMEM((EXAMPLES, side, width), jnp.float32),
            pltpu.VMEM((devices, 8, 128), jnp.float32),
            dma((8,)),
            dma((devices, pieces)),
            dma((4, devices, pieces)),
            dma((devices,)),
            dma((devices,)),
        ],
        compiler_params=pltpu.CompilerParams(
            collective_id=0, has_side_effects=True, vmem_limit_bytes=60 * 1024 * 1024
        ),
        cost_estimate=pl.CostEstimate(
            flops=2 * devices * rows * depth * 2 * width,
            bytes_accessed=2 * depth * width * 2,
            transcendentals=devices * rows * width,
        ),
    )(
        acts, out_grad, routes.T, route_weight.T, w_gate, w_up, proj_in.swapaxes(1, 2), proj_out.T
    )
    return scaled.reshape(1, EXAMPLES, side * side)


def solution(mesh):
    devices = mesh.shape["expert"]
    lines = 2 if devices == 16 else 1
    return jax.shard_map(
        functools.partial(on_device, devices, lines),
        mesh=mesh,
        in_specs=(
            P(("groups", "expert"), None),
            P(("groups", "expert"), None),
            P(("groups", "expert"), None),
            P(("groups", "expert"), None),
            P("expert", None, None),
            P("expert", None, None),
            P("expert", None, None),
            P(),
        ),
        out_specs=P("expert", "groups", None),
        check_vma=False,
    )
```

time: 71.5 us -> 70.1 us (0.980)
  local copies, waits for them, and re-layouts: 7.75 us -> 1.44 us
  Pallas kernels: 63.4 us -> 68.4 us
    unnamed x4 -> x0, local copies, waits for them, and re-layouts: 6.31 us -> none
    pallas_call x1, Pallas kernels: 63.4 us -> 68.4 us  [on_device(): pl.pallas_call(functools.partial(kernel, devices, lines), out_shape=jax.S...]
where the time goes in v2:
time: 70.1 us; the launch traced here: 69.9 us
  Pallas kernels  68.4 us (98%)
  local copies, waits for them, and re-layouts  1.44 us (2%)
    pallas_call x1, Pallas kernels, on_device(): pl.pallas_call(functools.partial(kernel, devices, lines), out_shape=jax.S...  68.4 us
    reshape x1, local copies, waits for them, and re-layouts, on_device(): return scaled.reshape(1, EXAMPLES, side * side)  1.44 us

profile of v2, /device:TPU:0, one launch (start us, length us, event | category | flops | bytes accessed | tf_op | source)
XLA Modules:
  0.0 69.9 jit_solution(1047130199273850454)
XLA Ops:
  0.0 68.4 %shard_map.82 = f32[2,32,32]{2,1,0:T(8,128)} custom-call(bf16[128,2048]{1,0:T(8,128)(2,1)} %acts_ref.1, bf16[128,2048]{1,0:T(8,128)(2,1)} %grad_ref.1, s32[8,128]{1,0:T(8,128)} %bitcast.6, f32[8,128]{1,0:T(8,128)} %bitcast.7, bf16[1,2048,768]{2,1,0:T(8,128)(2,1)} %gate_ref.1, bf16[1,2048,768]{2,1,0:T(8,128)(2,1)} %up_ref.1, bf16[1,32,768]{2,1,0:T(8,128)(2,1)} %bitcast.5, ...), custom_call_target="tpu_custom_call" | custom-call | flops 12884901888 | bytes 6291456 | tf_op jit(solution)/shard_map/pallas_call | solution.py:279
  68.5 1.4 %reshape.3 = f32[1,2,1024]{2,1,0:T(2,128)} reshape(f32[2,32,32]{2,1,0:T(8,128)} %shard_map.82) | data formatting | bytes 16384 | tf_op jit(solution)/shard_map/reshape | solution.py:313

commit v3 on v1

--- a/solution.py
+++ b/solution.py
@@ -13,26 +13,24 @@
 
 
 def row_chunks(rows, lines):
-    half = rows // 2
+    half, part = rows // 2, rows // 8
     if lines == 1:
         return ((0, half), (half, rows - half)), 2
-    late = rows // 8
-    return ((0, half), (half, rows - half - late), (rows - late, late)), 2
+    return ((0, 6 * part), (6 * part, part), (rows - part, part)), 2
 
 
 def kernel(
     devices, lines, acts_ref, grad_ref, routes_ref, weight_ref, gate_ref, up_ref, in_ref, out_ref,
     result_ref,
     acts, grad, routes, weight, gate, up, proj_in, proj_out,
-    sides_out, sides, total, powers,
-    local_sem, arrive_sem, send_sem, side_arrive, side_send, power_arrive, power_send,
+    notes, total, powers,
+    local_sem, arrive_sem, send_sem, power_arrive, power_send,
 ):
     length = devices // 2 // lines
     chips = devices // 2
     rows = acts.shape[1]
-    side = sides.shape[1]
+    side = proj_out.shape[0]
     width = gate.shape[1]
-    top = routes.shape[1]
     chunks, first_count = row_chunks(rows, lines)
     me = lax.axis_index("expert")
     core = lax.rem(me, 2)
@@ -59,15 +57,6 @@
     for load in loads:
         load.start()
 
-    barrier = pltpu.get_barrier_semaphore()
-
-    @pl.loop(1, devices)
-    def _(i):
-        other = lax.rem(me + i, devices)
-        pl.semaphore_signal(barrier, inc=1, device_id={"expert": other}, device_id_type=MESH)
-
-    pl.semaphore_wait(barrier, devices - 1)
-
     targets = (
         block(place + 1, line, core),
         block(place - 1, line, core),
@@ -78,18 +67,41 @@
     has_left = place > 0
     other_line = lines - 1 - line
 
+    neighbours = [(has_right, RIGHT), (has_left, LEFT), (True, SIBLING)]
+    if lines > 1:
+        neighbours.append((True, ACROSS))
+    barrier = pltpu.get_barrier_semaphore()
+    for present, way in neighbours:
+        @pl.when(present)
+        def _(way=way):
+            pl.semaphore_signal(
+                barrier, inc=1, device_id={"expert": targets[way]}, device_id_type=MESH
+            )
+
+    others = 1 + (lines - 1) + has_right.astype(jnp.int32) + has_left.astype(jnp.int32)
+    pl.semaphore_wait(barrier, others)
+
+    notes_chunk = len(chunks)
+
     def transfer(index, chunk, way, own=False):
-        start, count = chunks[chunk]
-        rows_of = pl.ds(start, count)
-        source = acts_ref.at[rows_of] if own else acts.at[index, rows_of]
+        if chunk == notes_chunk:
+            source = target = notes.at[index]
+        else:
+            start, count = chunks[chunk]
+            source = target = acts.at[index, pl.ds(start, count)]
+            if own:
+                source = acts_ref.at[pl.ds(start, count)]
         return pltpu.make_async_remote_copy(
             src_ref=source,
-            dst_ref=acts.at[index, rows_of],
+            dst_ref=target,
             send_sem=send_sem.at[way, index, chunk],
             recv_sem=arrive_sem.at[index, chunk],
             device_id={"expert": targets[way]},
             device_id_type=MESH,
         )
+
+    def own_notes():
+        return [(present, me, notes_chunk, way) for present, way in neighbours]
 
     def own_moves():
         moves = []
@@ -114,8 +126,8 @@
                 (present, index, chunk, SIBLING),
             ]
             listed.append((present, index, chunk, moves))
-        for chunk in range(len(chunks)):
-            late = chunk >= first_count
+        for chunk in (*range(first_count), notes_chunk, *range(first_count, len(chunks))):
+            late = first_count <= chunk < notes_chunk
             for way in (RIGHT, LEFT):
                 at = place - distance if way == RIGHT else place + distance
                 inside = (at >= 0) if way == RIGHT else (at < length)
@@ -151,39 +163,34 @@
 
     for load in loads[:4]:
         load.wait()
-    projected = jnp.dot(grad[...], proj_out[...], preferred_element_type=jnp.float32).T
-    names = routes[...].astype(jnp.float32).T
-    scales = weight[...].T
-
-    @pl.loop(0, devices)
-    def _(expert):
-        hit = names == lax.convert_element_type(expert, jnp.float32)
-        scale = jnp.sum(jnp.where(hit, scales, 0.0), axis=0, keepdims=True)
-        sides_out[expert] = (projected * scale).astype(jnp.bfloat16)
-
-    def side_move(other):
-        return pltpu.make_async_remote_copy(
-            src_ref=sides_out.at[other],
-            dst_ref=sides.at[me],
-            send_sem=side_send.at[other],
-            recv_sem=side_arrive.at[me],
-            device_id={"expert": other},
-            device_id_type=MESH,
+    projected = lax.dot_general(
+        proj_out[...], grad[...], (((1,), (1,)), ((), ())), preferred_element_type=jnp.float32
+    )
+    names = routes[...]
+    scales = weight[...]
+
+    notes[me, :side] = projected
+    for expert in range(devices):
+        hit = names == expert
+        notes[me, side + expert : side + expert + 1] = jnp.sum(
+            jnp.where(hit, scales, 0.0), axis=0, keepdims=True
         )
-
-    @pl.loop(1, devices)
-    def _(i):
-        side_move(lax.rem(me + i, devices)).start()
-
-    sides[me] = sides_out[me]
+    for present, index, chunk, way in own_notes():
+        @pl.when(present)
+        def _(index=index, chunk=chunk, way=way):
+            transfer(index, chunk, way).start()
+
     total[...] = jnp.zeros_like(total)
     for load in loads[4:]:
         load.wait()
 
     def compute(chip_index):
         x = acts[pl.ds(2 * chip_index, 2)].reshape(2 * rows, acts.shape[2])
-        pair = sides[pl.ds(2 * chip_index, 2)]
-        pair = jnp.concatenate([pair[0], pair[1]], axis=1)
+        pair = [
+            notes[2 * chip_index + part, :side] * notes[2 * chip_index + part, pl.ds(side + me, 1)]
+            for part in range(2)
+        ]
+        pair = jnp.concatenate(pair, axis=1).astype(jnp.bfloat16)
         example = chip_index // (chips // EXAMPLES)
         step = 256
         for start in range(0, width, step):
@@ -217,33 +224,23 @@
 
             @pl.when(present)
             def _():
-                for chunk in range(len(chunks)):
+                for chunk in range(len(chunks) + 1):
                     transfer(sibling_of(index), chunk, SIBLING).wait_recv()
-
-                pltpu.make_async_copy(
-                    sides.at[sibling_of(index)],
-                    sides.at[sibling_of(index)],
-                    side_arrive.at[sibling_of(index)],
-                ).wait()
-
-                @pl.when(index != me)
-                def _():
-                    pltpu.make_async_copy(
-                        sides.at[index], sides.at[index], side_arrive.at[index]
-                    ).wait()
 
                 compute(index // 2)
 
     raw = []
     matrix = proj_in[...].astype(jnp.float32)
     for example in range(EXAMPLES):
-        turned = jnp.dot(
-            total[example],
-            matrix,
-            preferred_element_type=jnp.float32,
-            precision=lax.Precision.HIGHEST,
+        raw.append(
+            lax.dot_general(
+                matrix,
+                total[example],
+                (((1,), (1,)), ((), ())),
+                preferred_element_type=jnp.float32,
+                precision=lax.Precision.HIGHEST,
+            )
         )
-        raw.append(turned.T)
     own_power = [jnp.sum(one * one, keepdims=True) for one in raw]
     row_of = lax.broadcasted_iota(jnp.int32, (8, 128), 0)
     tile = jnp.zeros((8, 128), jnp.float32)
@@ -261,11 +258,10 @@
             device_id_type=MESH,
         )
 
-    @pl.loop(1, devices)
-    def _(i):
+    for i in range(1, devices):
         power_move(lax.rem(me + i, devices)).start()
 
-    for present, index, chunk, way in own_moves():
+    for present, index, chunk, way in own_moves() + own_notes():
         @pl.when(present)
         def _(index=index, chunk=chunk, way=way):
             transfer(index, chunk, way, own=True).wait_send()
@@ -278,10 +274,8 @@
                 def _(index=index, chunk=chunk, way=way):
                     transfer(index, chunk, way).wait_send()
 
-    @pl.loop(1, devices)
-    def _(i):
+    for i in range(1, devices):
         other = lax.rem(me + i, devices)
-        side_move(other).wait_send()
         power_move(other).wait_send()
         pltpu.make_async_copy(powers.at[other], powers.at[other], power_arrive.at[other]).wait()
 
@@ -296,7 +290,7 @@
     top = routes.shape[1]
     width = w_gate.shape[2]
     side = proj_out.shape[1]
-    pieces = len(row_chunks(rows, lines)[0])
+    pieces = len(row_chunks(rows, lines)[0]) + 1
     dma = pltpu.SemaphoreType.DMA
     scaled = pl.pallas_call(
         functools.partial(kernel, devices, lines),
@@ -306,21 +300,18 @@
         scratch_shapes=[
             pltpu.VMEM((devices, rows, depth), jnp.bfloat16),
             pltpu.VMEM((rows, depth), jnp.bfloat16),
-            pltpu.VMEM((rows, top), jnp.int32),
-            pltpu.VMEM((rows, top), jnp.float32),
+            pltpu.VMEM((top, rows), jnp.int32),
+            pltpu.VMEM((top, rows), jnp.float32),
             pltpu.VMEM((depth, width), jnp.bfloat16),
             pltpu.VMEM((depth, width), jnp.bfloat16),
-            pltpu.VMEM((width, side), jnp.bfloat16),
-            pltpu.VMEM((depth, side), jnp.bfloat16),
-            pltpu.VMEM((devices, side, rows), jnp.bfloat16),
-            pltpu.VMEM((devices, side, rows), jnp.bfloat16),
+            pltpu.VMEM((side, width), jnp.bfloat16),
+            pltpu.VMEM((side, depth), jnp.bfloat16),
+            pltpu.VMEM((devices, side + devices, rows), jnp.float32),
             pltpu.VMEM((EXAMPLES, side, width), jnp.float32),
             pltpu.VMEM((devices, 8, 128), jnp.float32),
             dma((8,)),
             dma((devices, pieces)),
             dma((4, devices, pieces)),
-            dma((devices,)),
-            dma((devices,)),
             dma((devices,)),
             dma((devices,)),
         ],
@@ -332,7 +323,9 @@
             bytes_accessed=2 * depth * width * 2,
             transcendentals=devices * rows * width,
         ),
-    )(acts, out_grad, routes, route_weight, w_gate, w_up, proj_in, proj_out)
+    )(
+        acts, out_grad, routes.T, route_weight.T, w_gate, w_up, proj_in.swapaxes(1, 2), proj_out.T
+    )
     return scaled.reshape(1, EXAMPLES, side * side)
 
 

time: 71.5 us -> 64.4 us (0.901)
  local copies, waits for them, and re-layouts: 7.75 us -> 1.44 us
    unnamed x4 -> x0, local copies, waits for them, and re-layouts: 6.31 us -> none
where the time goes in v3:
time: 64.4 us; the launch traced here: 64.2 us
  Pallas kernels  62.8 us (98%)
  local copies, waits for them, and re-layouts  1.44 us (2%)
    pallas_call x1, Pallas kernels, on_device(): pl.pallas_call(functools.partial(kernel, devices, lines), out_shape=jax.S...  62.8 us
    reshape x1, local copies, waits for them, and re-layouts, on_device(): return scaled.reshape(1, EXAMPLES, side * side)  1.44 us

profile of v3, /device:TPU:0, one launch (start us, length us, event | category | flops | bytes accessed | tf_op | source)
XLA Modules:
  0.0 64.2 jit_solution(786764697460444369)
XLA Ops:
  0.0 62.8 %shard_map.82 = f32[2,32,32]{2,1,0:T(8,128)} custom-call(bf16[128,2048]{1,0:T(8,128)(2,1)} %acts_ref.1, bf16[128,2048]{1,0:T(8,128)(2,1)} %grad_ref.1, s32[8,128]{1,0:T(8,128)} %bitcast.6, f32[8,128]{1,0:T(8,128)} %bitcast.7, bf16[1,2048,768]{2,1,0:T(8,128)(2,1)} %gate_ref.1, bf16[1,2048,768]{2,1,0:T(8,128)(2,1)} %up_ref.1, bf16[1,32,768]{2,1,0:T(8,128)(2,1)} %bitcast.5, ...), custom_call_target="tpu_custom_call" | custom-call | flops 12884901888 | bytes 6291456 | tf_op jit(solution)/shard_map/pallas_call | solution.py:295
  62.8 1.4 %reshape.3 = f32[1,2,1024]{2,1,0:T(2,128)} reshape(f32[2,32,32]{2,1,0:T(8,128)} %shard_map.82) | data formatting | bytes 16384 | tf_op jit(solution)/shard_map/reshape | solution.py:329

commit v4 on v3

--- a/solution.py
+++ b/solution.py
@@ -16,7 +16,7 @@
     half, part = rows // 2, rows // 8
     if lines == 1:
         return ((0, half), (half, rows - half)), 2
-    return ((0, 6 * part), (6 * part, part), (rows - part, part)), 2
+    return ((0, half), (half, 3 * part), (rows - part, part)), 2
 
 
 def kernel(
@@ -156,10 +156,14 @@
                     listed.append((present, index, chunk, [(present, index, chunk, SIBLING)]))
         return listed
 
-    for present, index, chunk, way in own_moves():
-        @pl.when(present)
-        def _(index=index, chunk=chunk, way=way):
-            transfer(index, chunk, way, own=True).start()
+    def start_own(later):
+        for present, index, chunk, way in own_moves():
+            if later == (chunk > 0 and (way != ACROSS or chunk < first_count)):
+                @pl.when(present)
+                def _(index=index, chunk=chunk, way=way):
+                    transfer(index, chunk, way, own=True).start()
+
+    start_own(False)
 
     for load in loads[:4]:
         load.wait()
@@ -169,6 +173,7 @@
     names = routes[...]
     scales = weight[...]
 
+    start_own(True)
     notes[me, :side] = projected
     for expert in range(devices):
         hit = names == expert
@@ -282,7 +287,9 @@
     power = jnp.sum(powers[...], axis=0)
     factor = lax.rsqrt(power / (devices * side * side) + 1e-06)
     for example in range(EXAMPLES):
-        result_ref[example] = raw[example] * factor[example : example + 1, :1]
+        scaled = raw[example] * factor[example : example + 1, :1]
+        for row in range(side):
+            result_ref[0, example : example + 1, row * side : (row + 1) * side] = scaled[row : row + 1]
 
 
 def on_device(devices, lines, acts, out_grad, routes, route_weight, w_gate, w_up, proj_in, proj_out):
@@ -294,7 +301,7 @@
     dma = pltpu.SemaphoreType.DMA
     scaled = pl.pallas_call(
         functools.partial(kernel, devices, lines),
-        out_shape=jax.ShapeDtypeStruct((EXAMPLES, side, side), jnp.float32),
+        out_shape=jax.ShapeDtypeStruct((1, EXAMPLES, side * side), jnp.float32),
         in_specs=[pl.BlockSpec(memory_space=pl.ANY)] * 8,
         out_specs=pl.BlockSpec(memory_space=pltpu.VMEM),
         scratch_shapes=[
@@ -326,7 +333,7 @@
     )(
         acts, out_grad, routes.T, route_weight.T, w_gate, w_up, proj_in.swapaxes(1, 2), proj_out.T
     )
-    return scaled.reshape(1, EXAMPLES, side * side)
+    return scaled
 
 
 def solution(mesh):

time: 64.4 us -> 64.3 us (level)
    reshape x1 -> x0, local copies, waits for them, and re-layouts: 1.44 us -> none  [on_device(): return scaled.reshape(1, EXAMPLES, side * side)]
    unnamed x0 -> x1, local copies, waits for them, and re-layouts: none -> 1.3 us
where the time goes in v4:
time: 64.3 us; the launch traced here: 64.1 us
  Pallas kernels  62.8 us (98%)
  local copies, waits for them, and re-layouts  1.3 us (2%)
    pallas_call x1, Pallas kernels, on_device(): pl.pallas_call(functools.partial(kernel, devices, lines), out_shape=jax.S...  62.8 us
    unnamed x1, local copies, waits for them, and re-layouts  1.3 us

profile of v4, /device:TPU:0, one launch (start us, length us, event | category | flops | bytes accessed | tf_op | source)
XLA Modules:
  0.0 64.1 jit_solution(17891317200694617930)
XLA Ops:
  0.0 62.8 %shard_map.82 = f32[1,2,1024]{2,1,0:T(2,128)} custom-call(bf16[128,2048]{1,0:T(8,128)(2,1)} %acts_ref.1, bf16[128,2048]{1,0:T(8,128)(2,1)} %grad_ref.1, s32[8,128]{1,0:T(8,128)} %bitcast.6, f32[8,128]{1,0:T(8,128)} %bitcast.7, bf16[1,2048,768]{2,1,0:T(8,128)(2,1)} %gate_ref.1, bf16[1,2048,768]{2,1,0:T(8,128)(2,1)} %up_ref.1, bf16[1,32,768]{2,1,0:T(8,128)(2,1)} %bitcast.5, ...), custom_call_target="tpu_custom_call" | custom-call | flops 12884901888 | bytes 6291456 | tf_op jit(solution)/shard_map/pallas_call | solution.py:302
  62.8 1.3 %copy.10 = f32[1,2,1024]{2,1,0:T(2,128)} copy(f32[1,2,1024]{2,1,0:T(2,128)} %shard_map.82) | data formatting | bytes 16384
